TPU v7x, 32 devices: a whole 2x2x4 slice. The times are simulated.
32 devices in a mesh: section: 8 (over y, x, core), tensor: 4 (over z).
Axes of the slice: x: 2, y: 2, z: 4, core: 2. Of those that a mesh axis runs over, the one named last changes fastest.
Arguments:
- weights: bfloat16 [8, 4096, 4096], P('section', 'tensor'), may hold values from -0.09375 to 0.09375
- filters: float32 [8, 32, 128], P('section'), may hold values from -0.5 to 0.5
- down_input: bfloat16 [8, 512, 4096], P('section', 'tensor'), may hold values from -6 to 6
- down_cot: bfloat16 [8, 512, 4096], P('section', 'tensor'), may hold values from -6 to 6
- up_input: bfloat16 [8, 512, 4096], P('section', 'tensor'), may hold values from -6 to 6
- up_cot: bfloat16 [8, 512, 4096], P('section', 'tensor'), may hold values from -6 to 6
Outputs:
- weight_grad: bfloat16 [8, 4096, 4096], P('section', 'tensor')
- filter_grad: float32 [8, 32, 128], P('section')
- down_passed: bfloat16 [8, 512, 4096], P('section', 'tensor')
- up_passed: bfloat16 [8, 512, 4096], P('section', 'tensor')
All inputs are finite; a program needn't handle non-finite values.
Results may differ from a plain program's by a relative error of at most 0.014.
Values may be sent and summed in bfloat16 or wider, within the bound.
No kernel may reach another device: no remote copies, remote signals or barrier semaphores. Data moves between devices by JAX's collectives and lax.ppermute only.
A program may use at most 192 MiB of HBM per device.

v0:
```python
import jax
import jax.numpy as jnp
from jax import lax
from jax.sharding import PartitionSpec as P

epsilon = 1e-06


def shifted(x, axis, by):
    devices = lax.axis_size(axis)
    pairs = [(i, i + by) for i in range(devices) if 0 <= i + by < devices]
    return lax.ppermute(x, axis, pairs)


def tap_tables(row_count, taps_total):
    target = jnp.arange(row_count, dtype=jnp.int32)[:, None, None]
    source = jnp.arange(row_count + taps_total - 1, dtype=jnp.int32)[None, :, None]
    lag_index = jnp.arange(taps_total, dtype=jnp.int32)[None, None, :]
    causal_table = (target + taps_total - 1 - source == lag_index).astype(jnp.float32)
    ahead_table = (source - target == lag_index).astype(jnp.float32)
    return (causal_table, ahead_table)


def banded(table, filter_taps, extended, row_count):
    group_count = filter_taps.shape[0]
    band = jnp.einsum("tuk,gk->gtu", table, filter_taps, precision=lax.Precision.HIGHEST)
    grouped = extended.reshape(extended.shape[0], extended.shape[1], group_count, -1)
    mixed_out = jnp.einsum("gtu,umgc->tmgc", band, grouped, precision=lax.Precision.HIGHEST)
    return mixed_out.reshape(row_count, extended.shape[1], extended.shape[2])


def layer_grads(inputs, cotangent, weight_rows, filter_taps, tables):
    causal_table, ahead_table = tables
    row_count = inputs.shape[0]
    group_count = filter_taps.shape[0]
    taps_total = filter_taps.shape[1]
    input_wide = inputs.astype(jnp.float32)
    inverse_rms = lax.rsqrt(jnp.mean(input_wide * input_wide, axis=2, keepdims=True) + epsilon)
    normed = input_wide * inverse_rms
    normed_b = normed.astype(jnp.bfloat16)
    feature_rows = lax.all_to_all(normed_b, "tensor", split_axis=2, concat_axis=0, tiled=True)
    selected = feature_rows
    values = lax.psum_scatter(
        jnp.einsum("tmd,de->tme", selected, weight_rows, preferred_element_type=jnp.float32).astype(
            jnp.bfloat16
        ),
        "tensor",
        scatter_dimension=0,
        tiled=True,
    ).astype(jnp.float32)
    before = shifted(
        values[row_count - (taps_total - 1) :].astype(jnp.bfloat16), "tensor", 1
    ).astype(jnp.float32)
    extended = jnp.concatenate([before, values], axis=0)
    convolved = banded(causal_table, filter_taps, extended, row_count)
    cot_wide = cotangent.astype(jnp.float32)
    grad_mix = cot_wide * normed
    following = shifted(grad_mix[: taps_total - 1], "tensor", -1)
    grad_ext = jnp.concatenate([grad_mix, following], axis=0)
    grad_values = banded(ahead_table, filter_taps, grad_ext, row_count)
    grad_grouped = grad_mix.reshape(row_count, grad_mix.shape[1], group_count, -1)
    ext_grouped = extended.reshape(extended.shape[0], extended.shape[1], group_count, -1)
    pairs = jnp.einsum("tmgc,umgc->gtu", grad_grouped, ext_grouped, precision=lax.Precision.HIGHEST)
    tap_part = jnp.einsum("gtu,tuk->gk", pairs, causal_table, precision=lax.Precision.HIGHEST)
    grad_values_b = grad_values.astype(jnp.bfloat16)
    shard_rows = lax.all_gather(grad_values_b, "tensor", axis=0, tiled=True)
    selected = feature_rows
    weight_sum = jnp.einsum("tmd,tme->de", selected, shard_rows, preferred_element_type=jnp.float32)
    returned_rows = jnp.einsum(
        "tme,de->tmd", shard_rows, weight_rows, preferred_element_type=jnp.float32
    )
    back_tokens = lax.all_to_all(
        returned_rows.astype(jnp.bfloat16), "tensor", split_axis=0, concat_axis=2, tiled=True
    ).astype(returned_rows.dtype)
    grad_total = cot_wide * convolved + back_tokens
    projection_mean = jnp.mean(grad_total * normed, axis=2, keepdims=True)
    grad_in = (cot_wide + inverse_rms * (grad_total - normed * projection_mean)).astype(
        jnp.bfloat16
    )
    return (grad_in, weight_sum, tap_part)


def mirrored(stacked):
    sections = lax.axis_size("section")
    pieces = stacked.reshape(
        stacked.shape[0], stacked.shape[1], sections, stacked.shape[2] // sections
    )
    spread = lax.all_to_all(pieces, "section", split_axis=2, concat_axis=2, tiled=True)
    collected = lax.all_to_all(
        jnp.flip(spread, 2), "section", split_axis=2, concat_axis=2, tiled=True
    )
    return collected.reshape(stacked.shape)


def per_device(weights, filters, down_input, down_cot, up_input, up_cot):
    weight_rows = weights[0]
    filter_taps = filters[0]
    tables = tap_tables(down_input.shape[1], filter_taps.shape[1])
    arriving = mirrored(jnp.stack([up_input[0], up_cot[0]], axis=1))
    up_inputs = arriving[:, 0:1]
    up_cotangent = arriving[:, 1:2]
    down_inputs = down_input[0][:, None]
    down_cotangent = down_cot[0][:, None]
    down_result, down_weight, down_taps = layer_grads(
        down_inputs, down_cotangent, weight_rows, filter_taps, tables
    )
    up_grad, up_weight, up_taps = layer_grads(
        up_inputs, up_cotangent, weight_rows, filter_taps, tables
    )
    down_grad = down_result[:, 0]
    weight_part = down_weight + up_weight
    tap_part = down_taps + up_taps
    taps_total = lax.psum(tap_part, "tensor")
    down_passed = shifted(down_grad, "section", -1)
    up_passed = shifted(mirrored(up_grad)[:, 0], "section", 1)
    return (
        weight_part.astype(jnp.bfloat16)[None],
        taps_total[None],
        down_passed[None],
        up_passed[None],
    )


def solution(mesh):
    in_specs = (
        P("section", "tensor", None),
        P("section", None, None),
        P("section", "tensor", None),
        P("section", "tensor", None),
        P("section", "tensor", None),
        P("section", "tensor", None),
    )
    out_specs = (
        P("section", "tensor", None),
        P("section", None, None),
        P("section", "tensor", None),
        P("section", "tensor", None),
    )
    return jax.shard_map(
        per_device, mesh=mesh, in_specs=in_specs, out_specs=out_specs, check_vma=False
    )
```

profile of v0, /device:TPU:10, one launch (start us, length us, event | category | flops | bytes accessed | tf_op | source)
XLA Modules:
  0.0 725.9 jit_solution(2285130957430445176)
XLA Ops:
  22.0 7.8 %copy.99 = f32[127,1,4096]{2,1,0:T(1,128)} copy(f32[127,1,4096]{0,1,2:T(1,128)} %slice_multiply_fusion) | data formatting | bytes 4161536 | tf_op jit(solution)/shard_map/slice | solution.py:58
  40.3 14.0 %fusion.40 = f32[32,128,255]{1,0,2:T(8,128)} fusion(s32[128,255]{0,1:T(8,128)S(1)} %iota_subtract_fusion.1, f32[1,32,128]{2,1,0:T(8,128)S(1)} %copy-done), kind=kOutput, calls=%fused_computation.42 | convolution fusion | flops 1608499200 | bytes 4324864 | tf_op jit(solution)/shard_map/tuk,gk->gtu/dot_general | solution.py:26
  59.5 5.9 all-to-all-done.1
  66.9 5.7 all-to-all-start.2
  72.7 6.3 collective-permute-done
  79.0 5.7 copy.100
  84.7 8.0 %fusion.60 = bf16[32,128,128]{2,1,0:T(8,128)(2,1)} fusion(f32[32,128,255]{2,1,0:T(8,128)} %copy.101, f32[127,1,32,128]{0,3,2,1:T(8,128)} %bitcast.229, f32[128,1,32,128]{0,3,2,1:T(8,128)S(1)} %copy-done.10), kind=kOutput, calls=%fused_computation.72 | convolution fusion | flops 1605890048 | bytes 9404416 | tf_op jit(solution)/shard_map/gtu,umgc->tmgc/dot_general | solution.py:28
  102.3 5.7 copy.107
  110.1 103.5 %collective-permute-done.1 = f32[127,1,4096]{2,1,0:T(1,128)} collective-permute-done((f32[127,1,4096]{2,1,0:T(1,128)}, f32[127,1,4096]{2,1,0:T(1,128)}, u32[]{:S(2)}, u32[]{:S(2)}) %collective-permute-start.1) | collective-permute-done | bytes 2080800 | tf_op jit(solution)/shard_map/ppermute | solution.py:12
  213.6 5.6 copy.108
  232.9 24.5 %reduce.6 = bf16[4096,128]{1,0:T(8,128)(2,1)} reduce(bf16[4096,1,128]{2,1,0:T(2,128)(2,1)} %bitcast.226, bf16[]{:T(256)} %broadcast.137), dimensions={1}, to_apply=%bitcast.203.reduce_sub_computation | reduce | bytes 2097154
  260.8 54.8 %all_to_all.68 = bf16[4,2,65536]{2,1,0:T(2,128)(2,1)} all-to-all(bf16[4,2,65536]{2,1,0:T(2,128)(2,1)} %reshape.474), channel_id=1, replica_groups=mesh['section'=8,'tensor'=4] {'tensor'}, dimensions={0} | all-to-all | bytes 2097152 | tf_op jit(solution)/shard_map/all_to_all | solution.py:41
  324.5 10.2 %fusion.23 = bf16[512,1,4096]{2,0,1:T(8,128)(2,1)} fusion(bf16[512,1024]{1,0:T(8,128)(2,1)} %bitcast.237, bf16[1,1024,4096]{2,1,0:T(8,128)(2,1)} %param.6), kind=kOutput, calls=%fused_computation.22 | convolution fusion | flops 4297064448 | bytes 13631488 | tf_op jit(solution)/shard_map/tmd,de->tme/dot_general | solution.py:44
  334.8 24.4 %reduce.5 = bf16[4096,128]{1,0:T(8,128)(2,1)} reduce(bf16[4096,1,128]{2,1,0:T(2,128)(2,1)} %bitcast.223, bf16[]{:T(256)} %broadcast.137), dimensions={1}, to_apply=%bitcast.182.reduce_sub_computation | reduce | bytes 2097154
  362.7 59.7 %all_to_all.69 = bf16[4,2,65536]{2,1,0:T(2,128)(2,1)} all-to-all(bf16[4,2,65536]{2,1,0:T(2,128)(2,1)} %reshape.472), channel_id=1, replica_groups=mesh['section'=8,'tensor'=4] {'tensor'}, dimensions={0} | all-to-all | bytes 2097152 | tf_op jit(solution)/shard_map/all_to_all | solution.py:41
  431.4 10.3 %fusion.26 = bf16[512,1,4096]{2,0,1:T(8,128)(2,1)} fusion(bf16[512,1024]{1,0:T(8,128)(2,1)} %bitcast.239, bf16[1,1024,4096]{2,1,0:T(8,128)(2,1)} %param.6), kind=kOutput, calls=%fused_computation.23 | convolution fusion | flops 4297064448 | bytes 13631488 | tf_op jit(solution)/shard_map/tmd,de->tme/dot_general | solution.py:44
  441.7 10.2 %fusion.76 = bf16[512,1,1024]{2,0,1:T(8,128)(2,1)} fusion(bf16[1,1024,4096]{2,1,0:T(8,128)(2,1)} %param.6, bf16[512,1,4096]{0,2,1:T(8,128)(2,1)} %all-gather.3.cloned.1.call-done), kind=kOutput, calls=%fused_computation.77 | convolution fusion | flops 4295491584 | bytes 13631488 | tf_op jit(solution)/shard_map/tme,de->tmd/dot_general | solution.py:69
  459.0 7.1 all-to-all-start.4
  466.1 10.3 %fusion.71 = bf16[512,1,1024]{2,0,1:T(8,128)(2,1)} fusion(bf16[1,1024,4096]{2,1,0:T(8,128)(2,1)} %param.6, bf16[512,1,4096]{0,2,1:T(8,128)(2,1)} %all-gather.5.cloned.1.call-done), kind=kOutput, calls=%fused_computation.76 | convolution fusion | flops 4295491584 | bytes 13631488 | tf_op jit(solution)/shard_map/tme,de->tmd/dot_general | solution.py:69
  483.4 33.7 %all-to-all-done.4 = bf16[4,2,65536]{2,1,0:T(2,128)(2,1)} async-done(((bf16[4,2,65536]{2,1,0:T(2,128)(2,1)}), bf16[4,2,65536]{2,1,0:T(2,128)(2,1)}, u32[]{:S(2)}, u32[]{:S(2)}) %all-to-all-start.4) | async-done | bytes 1048608 | tf_op jit(solution)/shard_map/all_to_all | solution.py:72
  517.1 7.7 %all-to-all-start.5 = ((bf16[4,2,65536]{2,1,0:T(2,128)(2,1)}), bf16[4,2,65536]{2,1,0:T(2,128)(2,1)}, u32[]{:S(2)}, u32[]{:S(2)}) async-start(bf16[4,2,65536]{2,1,0:T(2,128)(2,1)} %reshape.478), calls=%async_computation.7 | async-start | bytes 2097152 | tf_op jit(solution)/shard_map/all_to_all | solution.py:72
  524.8 13.9 %fusion.41 = f32[32,128,255]{1,0,2:T(8,128)} fusion(s32[128,255]{0,1:T(8,128)S(1)} %iota_subtract_fusion, f32[1,32,128]{2,1,0:T(8,128)S(1)} %copy-done), kind=kOutput, calls=%fused_computation.43 | convolution fusion | flops 1608499200 | bytes 4324864 | tf_op jit(solution)/shard_map/tuk,gk->gtu/dot_general | solution.py:26
  555.8 10.4 %fusion.35 = f32[1024,4096]{1,0:T(8,128)} fusion(bf16[512,1024]{1,0:T(8,128)(2,1)S(1)} %bitcast.240, bf16[512,1,4096]{0,2,1:T(8,128)(2,1)} %all-gather.3.cloned.1.call-done), kind=kOutput, calls=%fused_computation.32 | convolution fusion | flops 4294967296 | bytes 22020096 | tf_op jit(solution)/shard_map/tmd,tme->de/dot_general | solution.py:68
  570.3 6.1 copy.120
  586.3 6.1 copy.124
  619.1 8.0 %fusion.54 = (f32[128]{0:T(128)S(1)}, f32[32,128,128]{2,1,0:T(8,128)}) fusion(f32[128,1,32,128]{0,3,2,1:T(8,128)} %bitcast.219, f32[128,1,32,128]{0,3,2,1:T(8,128)S(1)} %bitcast.211, f32[128,1,32,128]{0,3,2,1:T(8,128)} %bitcast.213, f32[128]{0:T(128)S(1)} %add_rsqrt_fusion.1, bf16[255,32,128]{0,2,1:T(8,128)(2,1)} %bitcast.220, f32[32,128,255]{2,1,0:T(8,128)} %copy.118), kind=kOutput, calls=%fused_computation.63 | convolution fusion | flops 1606942592 | bytes 14656512 | tf_op jit(solution)/shard_map/gtu,umgc->tmgc/dot_general | solution.py:28
  644.2 5.4 copy.113
  649.6 11.2 %fusion.81 = f32[32,128]{1,0:T(8,128)S(1)} fusion(f32[32,128,255]{1,0,2:T(8,128)} %copy.113, s32[128,255]{0,1:T(8,128)S(1)} %iota_subtract_fusion), kind=kOutput, calls=%fused_computation.78 | convolution fusion | flops 1608499200 | bytes 4324864 | tf_op jit(solution)/shard_map/gtu,tuk->gk/dot_general | solution.py:64
  665.5 11.4 %fusion.4 = bf16[1,1024,4096]{2,1,0:T(8,128)(2,1)} fusion(f32[1024,4096]{1,0:T(8,128)} %fusion.35, bf16[512,1024]{1,0:T(8,128)(2,1)S(1)} %bitcast.238, bf16[512,1,4096]{0,2,1:T(8,128)(2,1)} %all-gather.5.cloned.1.call-done), kind=kOutput, calls=%fused_computation.7 | convolution fusion | flops 4303355904 | bytes 30408704 | tf_op jit(solution)/shard_map/tmd,tme->de/dot_general | solution.py:68
  684.3 5.5 copy.116
  689.8 11.2 %fusion.84 = f32[1,32,128]{2,1,0:T(8,128)S(1)} fusion(f32[32,128]{1,0:T(8,128)S(1)} %fusion.81, f32[32,128,255]{1,0,2:T(8,128)} %copy.116, s32[128,255]{0,1:T(8,128)S(1)} %iota_subtract_fusion), kind=kOutput, calls=%fused_computation.81 | convolution fusion | flops 1608503296 | bytes 4341248 | tf_op jit(solution)/shard_map/gtu,tuk->gk/dot_general | solution.py:64
  701.0 15.7 %psum.7 = f32[1,32,128]{2,1,0:T(8,128)} all-reduce(f32[1,32,128]{2,1,0:T(8,128)S(1)} %fusion.84), channel_id=1, replica_groups=mesh['section'=8,'tensor'=4] {'tensor'}, use_global_device_ids=true, to_apply=%region_4.5 | all-reduce | flops 4096 | bytes 32768 | tf_op jit(solution)/shard_map/psum | solution.py:113
  (124 shorter events, 185.3 us)
Async XLA Ops:
  7.2 33.1 %copy-start = (f32[1,32,128]{2,1,0:T(8,128)S(1)}, f32[1,32,128]{2,1,0:T(8,128)}, u32[]{:S(2)}) copy-start(f32[1,32,128]{2,1,0:T(8,128)} %param.7) | copy-start | bytes 49156
  12.1 3.2 copy-start.5
  15.3 3.4 copy-start.3
  22.0 10.2 %copy-start.15 = (bf16[1,128,4096]{2,1,0:T(8,128)(2,1)S(1)}, bf16[1,128,4096]{2,1,0:T(8,128)(2,1)}, u32[]{:S(2)}) copy-start(bf16[1,128,4096]{2,1,0:T(8,128)(2,1)} %param.10) | copy-start | bytes 3145732
  29.8 49.2 %collective-permute-start = (f32[127,1,4096]{2,1,0:T(1,128)}, f32[127,1,4096]{2,1,0:T(1,128)}, u32[]{:S(2)}, u32[]{:S(2)}) collective-permute-start(f32[127,1,4096]{2,1,0:T(1,128)} %copy.99), channel_id=1, source_target_pairs={{1,0},{2,1},{3,2},{5,4},{6,5},{7,6},{9,8},{10,9},{11,10},{13,12},{... | collective-permute-start | bytes 6242312 | tf_op jit(solution)/shard_map/ppermute | solution.py:12
  36.0 29.4 %all-to-all-start.1 = ((bf16[128,2,8,512]{0,3,1,2:T(8,128)(2,1)}), bf16[128,2,8,512]{0,3,1,2:T(8,128)(2,1)S(1)}, u32[]{:S(2)}, u32[]{:S(2)}) async-start(bf16[128,2,8,512]{0,3,1,2:T(8,128)(2,1)} %pad_maximum_fusion.1), calls=%async_computation.1 | async-start | bytes 4194304 | tf_op jit(solution)/shard_map/all_to_all | solution.py:88
  66.9 31.0 %all-to-all-start.2 = ((bf16[128,2,8,512]{0,3,1,2:T(8,128)(2,1)}), bf16[128,2,8,512]{0,3,1,2:T(8,128)(2,1)}, u32[]{:S(2)}, u32[]{:S(2)}) async-start(bf16[128,2,8,512]{0,3,1,2:T(8,128)(2,1)} %rev.8), calls=%async_computation.2 | async-start | bytes 4194304 | tf_op jit(solution)/shard_map/all_to_all | solution.py:89
  72.7 12.0 %copy-start.10 = (f32[128,1,32,128]{0,3,2,1:T(8,128)S(1)}, f32[128,1,32,128]{0,3,2,1:T(8,128)}, u32[]{:S(2)}) copy-start(f32[128,1,32,128]{0,3,2,1:T(8,128)} %get-tuple-element.16) | copy-start | bytes 6291460
  72.7 369.0 %all-gather.3.cloned.1.call-start = ((), (), s32[]{:S(2)}) async-start(), calls=%async_computation.10 | async-start | bytes 5242880 | tf_op jit(solution)/shard_map/all_gather | solution.py:66
  92.7 373.4 %all-gather.5.cloned.1.call-start = ((), (), s32[]{:S(2)}) async-start(), calls=%async_computation.11 | async-start | bytes 5242880 | tf_op jit(solution)/shard_map/all_gather | solution.py:66
  108.0 105.6 %collective-permute-start.1 = (f32[127,1,4096]{2,1,0:T(1,128)}, f32[127,1,4096]{2,1,0:T(1,128)}, u32[]{:S(2)}, u32[]{:S(2)}) collective-permute-start(f32[127,1,4096]{2,1,0:T(1,128)} %copy.107), channel_id=1, source_target_pairs={{1,0},{2,1},{3,2},{5,4},{6,5},{7,6},{9,8},{10,9},{11,10},{13,12},{... | collective-permute-start | bytes 6242312 | tf_op jit(solution)/shard_map/ppermute | solution.py:12
  219.3 3.4 copy-start.2
  228.0 321.9 %reduce-scatter.5.cloned.1.call-start = ((), (), s32[]{:S(2)}) async-start(), calls=%async_computation.13 | async-start | bytes 5242880 | tf_op jit(solution)/shard_map/reduce_scatter | solution.py:43
  334.7 241.6 %reduce-scatter.3.cloned.1.call-start = ((), (), s32[]{:S(2)}) async-start(), calls=%async_computation.12 | async-start | bytes 5242880 | tf_op jit(solution)/shard_map/reduce_scatter | solution.py:43
  459.0 58.2 %all-to-all-start.4 = ((bf16[4,2,65536]{2,1,0:T(2,128)(2,1)}), bf16[4,2,65536]{2,1,0:T(2,128)(2,1)}, u32[]{:S(2)}, u32[]{:S(2)}) async-start(bf16[4,2,65536]{2,1,0:T(2,128)(2,1)} %reshape.476), calls=%async_computation.6 | async-start | bytes 2097152 | tf_op jit(solution)/shard_map/all_to_all | solution.py:72
  517.1 65.2 %all-to-all-start.5 = ((bf16[4,2,65536]{2,1,0:T(2,128)(2,1)}), bf16[4,2,65536]{2,1,0:T(2,128)(2,1)}, u32[]{:S(2)}, u32[]{:S(2)}) async-start(bf16[4,2,65536]{2,1,0:T(2,128)(2,1)} %reshape.478), calls=%async_computation.7 | async-start | bytes 2097152 | tf_op jit(solution)/shard_map/all_to_all | solution.py:72
  549.9 5.9 copy-start.17
  552.4 40.0 %collective-permute-start.3 = (bf16[127,1,4096]{2,0,1:T(8,128)(2,1)}, bf16[127,1,4096]{2,0,1:T(8,128)(2,1)}, u32[]{:S(2)}, u32[]{:S(2)}) collective-permute-start(bf16[127,1,4096]{2,0,1:T(8,128)(2,1)} %slice.32), channel_id=1, source_target_pairs={{0,1},{1,2},{2,3},{4,5},{5,6},{6,7},{8,9},{9,10},{10,11},{12,13},{... | collective-permute-start | bytes 3121160 | tf_op jit(solution)/shard_map/ppermute | solution.py:12
  578.8 33.2 %collective-permute-start.2 = (bf16[127,1,4096]{2,0,1:T(8,128)(2,1)}, bf16[127,1,4096]{2,0,1:T(8,128)(2,1)}, u32[]{:S(2)}, u32[]{:S(2)}) collective-permute-start(bf16[127,1,4096]{2,0,1:T(8,128)(2,1)} %slice.31), channel_id=1, source_target_pairs={{0,1},{1,2},{2,3},{4,5},{5,6},{6,7},{8,9},{9,10},{10,11},{12,13},{... | collective-permute-start | bytes 3121160 | tf_op jit(solution)/shard_map/ppermute | solution.py:12
  599.6 5.3 copy-start.7
  607.2 4.8 copy-start.13
  607.2 19.9 %all-to-all-start.6 = ((bf16[128,1,8,512]{0,3,1,2:T(8,128)(2,1)}), bf16[128,1,8,512]{0,3,1,2:T(8,128)(2,1)}, u32[]{:S(2)}, u32[]{:S(2)}) async-start(bf16[128,1,8,512]{0,3,1,2:T(8,128)(2,1)} %bitcast.234), calls=%async_computation.8 | async-start | bytes 2097152 | tf_op jit(solution)/shard_map/all_to_all | solution.py:88
  614.9 4.2 copy-start.4
  627.1 7.0 copy-start.8
  629.6 31.3 %all-to-all-start.7 = ((bf16[128,1,8,512]{0,3,1,2:T(8,128)(2,1)}), bf16[128,1,8,512]{0,3,1,2:T(8,128)(2,1)}, u32[]{:S(2)}, u32[]{:S(2)}) async-start(bf16[128,1,8,512]{0,3,1,2:T(8,128)(2,1)} %rev.9), calls=%async_computation.9 | async-start | bytes 2097152 | tf_op jit(solution)/shard_map/all_to_all | solution.py:89
  634.1 6.2 copy-start.9
  634.1 6.2 copy-start.11
  634.1 6.2 copy-start.12
  638.0 38.9 %collective-permute-start.4 = (bf16[128,4096]{0,1:T(8,128)(2,1)}, bf16[128,4096]{0,1:T(8,128)(2,1)S(1)}, u32[]{:S(2)}, u32[]{:S(2)}) collective-permute-start(bf16[128,4096]{0,1:T(8,128)(2,1)} %fusion.51), channel_id=1, source_target_pairs={{4,0},{8,4},{12,8},{16,12},{20,16},{24,20},{28,24},{5,1},{9,5},{13... | collective-permute-start | bytes 3145736 | tf_op jit(solution)/shard_map/ppermute | solution.py:12
  660.8 4.7 copy-start.16
  663.2 53.5 %collective-permute-start.5 = (bf16[128,4096]{1,0:T(8,128)(2,1)}, bf16[128,4096]{1,0:T(8,128)(2,1)}, u32[]{:S(2)}, u32[]{:S(2)}) collective-permute-start(bf16[128,4096]{1,0:T(8,128)(2,1)} %copy.126), channel_id=1, source_target_pairs={{0,4},{4,8},{8,12},{12,16},{16,20},{20,24},{24,28},{1,5},{5,9},{9,... | collective-permute-start | bytes 3145736 | tf_op jit(solution)/shard_map/ppermute | solution.py:12
  689.8 29.1 %copy-start.1 = (f32[1,32,128]{2,1,0:T(8,128)S(1)}, f32[1,32,128]{2,1,0:T(8,128)}, u32[]{:S(2)}) copy-start(f32[1,32,128]{2,1,0:T(8,128)} %param.7) | copy-start | bytes 49156
  (2 other events, 4.0 us)
Sparse Core Ops, SparseCore 0:
  92.8 113.3 all-gather.2
  228.1 102.9 all-gather.4
  334.9 100.3 reduce-scatter.4
  441.8 121.6 reduce-scatter.2
where the time goes:
time: 741 us; the launch traced here: 726 us
  waiting for transfers between devices  155 us (21%)
  matrix products  149 us (20%)
  local copies, waits for them, and re-layouts  141 us (19%)
  blocking collectives  130 us (18%)
  other arithmetic  86.3 us (12%)
  starting transfers between devices  50.2 us (7%)
  between operations  14.5 us (2%)
    all_to_all x2, blocking collectives, layer_grads(): lax.all_to_all(normed_b, 'tensor', split_axis=2, concat_axis=0, tiled=True)  115 us
    ppermute x6, waiting for transfers between devices, shifted(): return lax.ppermute(x, axis, pairs)  110 us
    unnamed x2, other arithmetic  48.9 us
    unnamed x53, local copies, waits for them, and re-layouts  46.5 us
    all_to_all x2, waiting for transfers between devices, layer_grads(): lax.all_to_all(returned_rows.astype(jnp.bfloat16), 'tensor', split_axis=0...  33.7 us
    dot_general x2, matrix products, banded(): jnp.einsum('tuk,gk->gtu', table, filter_taps, precision=lax.Precision.HIG...  27.8 us
    dot_general x4, matrix products, banded(): jnp.einsum('gtu,umgc->tmgc', band, grouped, precision=lax.Precision.HIGHEST)  26.5 us
    dot_general x2, matrix products, layer_grads(): jnp.einsum('gtu,tuk->gk', pairs, causal_table, precision=lax.Precision.HI...  22.3 us
  transfers between devices with their start and end apart: 16, of which 5 were waited for; matrix products, arithmetic and copies ran while one was open for 48% of the time, Pallas kernels for 0%

commit v1 on v0

v1 whole, which is shorter than its diff:
```python
import functools

import jax
import jax.numpy as jnp
from jax import lax
from jax.experimental import pallas as pl
from jax.experimental.pallas import tpu as pltpu
from jax.sharding import PartitionSpec as P

epsilon = 1e-06
params = functools.partial(pltpu.CompilerParams, vmem_limit_bytes=40 * 1024 * 1024)
f32, bf16 = jnp.float32, jnp.bfloat16


def dot(a, b, dims=((1,), (0,))):
    return lax.dot_general(a, b, (dims, ((), ())), preferred_element_type=f32)


def shape(dims, dtype):
    return jax.ShapeDtypeStruct(dims, dtype)


def toeplitz_kernel(filters_ref, causal_ref, ahead_ref):
    taps = filters_ref.shape[1]
    row = lax.broadcasted_iota(jnp.int32, (taps, taps), 0)
    col = lax.broadcasted_iota(jnp.int32, (taps, taps), 1)
    for g in range(filters_ref.shape[0]):
        line = jnp.broadcast_to(filters_ref[g : g + 1, :], (taps, taps))
        turned = pltpu.roll(line, 0, 1, stride=1, stride_axis=0)
        own = jnp.where(col >= row, turned, 0.0)
        beyond = jnp.where(col < row, turned, 0.0)
        ahead_ref[g, :, :taps] = own.astype(bf16)
        ahead_ref[g, :, taps:] = beyond.astype(bf16)
        causal_ref[g, :, :taps] = beyond.T.astype(bf16)
        causal_ref[g, :, taps:] = own.T.astype(bf16)


def toeplitz(filters):
    groups, taps = filters.shape
    step = 8
    out = shape((groups, taps, 2 * taps), bf16)
    spec = pl.BlockSpec((step, taps, 2 * taps), lambda i: (i, 0, 0))
    return pl.pallas_call(
        toeplitz_kernel,
        grid=(groups // step,),
        in_specs=[pl.BlockSpec((step, taps), lambda i: (i, 0))],
        out_specs=[spec, spec],
        out_shape=[out, out],
        compiler_params=params(),
        name="toeplitz",
    )(filters)


def prepare_kernel(xin_ref, cot_ref, normed_ref, mix_ref):
    wide = xin_ref[...].astype(f32)
    inverse = lax.rsqrt(jnp.mean(wide * wide, axis=1, keepdims=True) + epsilon)
    normed = wide * inverse
    mix_ref[...] = (cot_ref[...].astype(f32) * normed).astype(bf16)
    width = normed_ref.shape[2]
    for i in range(normed_ref.shape[0]):
        normed_ref[i] = normed[:, i * width : (i + 1) * width].astype(bf16)


def prepare(xin, cot, blocks):
    rows, width = xin.shape
    step = 32
    spec = pl.BlockSpec((step, width), lambda i: (i, 0))
    return pl.pallas_call(
        prepare_kernel,
        grid=(rows // step,),
        in_specs=[spec, spec],
        out_specs=[pl.BlockSpec((blocks, step, width // blocks), lambda i: (0, i, 0)), spec],
        out_shape=[shape((blocks, rows, width // blocks), bf16), shape((rows, width), bf16)],
        compiler_params=params(),
        name="prepare",
    )(xin, cot)


def project_kernel(normed_ref, weight_ref, causal_ref, part_ref, mixed_ref):
    taps = causal_ref.shape[1]
    groups = causal_ref.shape[0]
    part = dot(normed_ref[...], weight_ref[...]).astype(bf16)
    part_ref[...] = part
    width = part.shape[1] // groups
    for g in range(groups):
        cols = slice(g * width, (g + 1) * width)
        for start in range(0, part.shape[0], taps):
            if start == 0:
                out = dot(causal_ref[g, :, taps:], part[:taps, cols])
            else:
                out = dot(causal_ref[g], part[start - taps : start + taps, cols])
            mixed_ref[start : start + taps, cols] = out.astype(bf16)


def project(normed, weight, causal):
    tokens, depth = normed.shape
    width = weight.shape[1]
    groups, taps, _ = causal.shape
    step = 4
    tile = width // groups * step
    spec = pl.BlockSpec((tokens, tile), lambda i: (0, i))
    return pl.pallas_call(
        project_kernel,
        grid=(groups // step,),
        in_specs=[
            pl.BlockSpec((tokens, depth), lambda i: (0, 0)),
            pl.BlockSpec((depth, tile), lambda i: (0, i)),
            pl.BlockSpec((step, taps, 2 * taps), lambda i: (i, 0, 0)),
        ],
        out_specs=[spec, spec],
        out_shape=[shape((tokens, width), bf16)] * 2,
        compiler_params=params(),
        name="project",
    )(normed, weight, causal)


def back_kernel(mix_ref, part_ref, weight_ref, ahead_ref, grad_ref, back_ref, taps_ref, total):
    groups, taps, _ = ahead_ref.shape
    tokens = mix_ref.shape[0]
    width = mix_ref.shape[1] // groups
    row = lax.broadcasted_iota(jnp.int32, (taps, taps), 0)
    col = lax.broadcasted_iota(jnp.int32, (taps, taps), 1)
    starts = range(0, tokens, taps)
    for g in range(groups):
        cols = slice(g * width, (g + 1) * width)
        mix = mix_ref[:, cols]
        part = part_ref[:, cols]
        for start in starts:
            if start + taps == tokens:
                out = dot(ahead_ref[g, :, :taps], mix[start:])
            else:
                out = dot(ahead_ref[g], mix[start : start + 2 * taps])
            grad_ref[start : start + taps, cols] = out.astype(bf16)
        mixes = jnp.concatenate([mix[s : s + taps] for s in starts], axis=1)
        parts = jnp.concatenate([part[s : s + taps] for s in starts], axis=1)
        same = dot(parts, mixes, ((1,), (1,)))
        later = dot(parts[:, :-width], mixes[:, width:], ((1,), (1,)))
        pairs = jnp.where(col >= row, same, later)
        folded = pairs[0:8]
        for a in range(8, taps, 8):
            folded = folded + pltpu.roll(pairs[a : a + 8], taps - a, 1)
        line = folded[0:1]
        for b in range(1, 8):
            line = line + pltpu.roll(folded[b : b + 1], taps - b, 1)
        taps_ref[0, g : g + 1, :] = line
    product = dot(grad_ref[...], weight_ref[...], ((1,), (1,)))
    step = pl.program_id(0)

    @pl.when(step == 0)
    def _():
        total[...] = product

    @pl.when(step > 0)
    def _():
        total[...] += product

    @pl.when(step == pl.num_programs(0) - 1)
    def _():
        back_ref[...] = total[...].astype(bf16)


def back(mix, part, weight, ahead):
    tokens, width = mix.shape
    depth = weight.shape[0]
    groups, taps, _ = ahead.shape
    step = 4
    tile = width // groups * step
    spec = pl.BlockSpec((tokens, tile), lambda i: (0, i))
    return pl.pallas_call(
        back_kernel,
        grid=(groups // step,),
        in_specs=[
            spec,
            spec,
            pl.BlockSpec((depth, tile), lambda i: (0, i)),
            pl.BlockSpec((step, taps, 2 * taps), lambda i: (i, 0, 0)),
        ],
        out_specs=[
            spec,
            pl.BlockSpec((tokens, depth), lambda i: (0, 0)),
            pl.BlockSpec((1, step, taps), lambda i: (i, 0, 0)),
        ],
        out_shape=[
            shape((tokens, width), bf16),
            shape((tokens, depth), bf16),
            shape((groups // step, step, taps), f32),
        ],
        scratch_shapes=[pltpu.VMEM((tokens, depth), f32)],
        compiler_params=params(),
        name="back",
    )(mix, part, weight, ahead)


def weight_kernel(down_x, up_x, down_g, up_g, out_ref, down_t, up_t):
    @pl.when(pl.program_id(0) == 0)
    def _():
        down_t[...] = down_x[...].T
        up_t[...] = up_x[...].T

    out_ref[...] = (dot(down_t[...], down_g[...]) + dot(up_t[...], up_g[...])).astype(bf16)


def weight_gradient(down_x, up_x, down_g, up_g):
    tokens, depth = down_x.shape
    width = down_g.shape[1]
    tile = width // 8
    whole = pl.BlockSpec((tokens, depth), lambda i: (0, 0))
    part = pl.BlockSpec((tokens, tile), lambda i: (0, i))
    return pl.pallas_call(
        weight_kernel,
        grid=(width // tile,),
        in_specs=[whole, whole, part, part],
        out_specs=pl.BlockSpec((depth, tile), lambda i: (0, i)),
        out_shape=shape((depth, width), bf16),
        scratch_shapes=[pltpu.VMEM((depth, tokens), bf16)] * 2,
        compiler_params=params(),
        name="weight_gradient",
    )(down_x, up_x, down_g, up_g)


def finish_kernel(xin_ref, cot_ref, mixed_ref, back_ref, out_ref):
    wide = xin_ref[...].astype(f32)
    inverse = lax.rsqrt(jnp.mean(wide * wide, axis=1, keepdims=True) + epsilon)
    normed = wide * inverse
    cot = cot_ref[...].astype(f32)
    returned = jnp.concatenate([back_ref[i] for i in range(back_ref.shape[0])], axis=1)
    total = cot * mixed_ref[...].astype(f32) + returned.astype(f32)
    mean = jnp.mean(total * normed, axis=1, keepdims=True)
    out_ref[...] = (cot + inverse * (total - normed * mean)).astype(bf16)


def finish(xin, cot, mixed, returned):
    rows, width = xin.shape
    blocks, _, depth = returned.shape
    step = 32
    spec = pl.BlockSpec((step, width), lambda i: (i, 0))
    return pl.pallas_call(
        finish_kernel,
        grid=(rows // step,),
        in_specs=[spec, spec, spec, pl.BlockSpec((blocks, step, depth), lambda i: (0, i, 0))],
        out_specs=spec,
        out_shape=shape((rows, width), bf16),
        compiler_params=params(),
        name="finish",
    )(xin, cot, mixed, returned)


def exchange(x):
    return lax.all_to_all(x, "tensor", split_axis=0, concat_axis=0, tiled=True)


def forward_half(xin, cot, weight, causal):
    blocks = lax.axis_size("tensor")
    normed, mix = prepare(xin, cot, blocks)
    features = exchange(normed)
    features = features.reshape(blocks * xin.shape[0], -1)
    mixes = lax.all_gather(mix, "tensor", axis=0, tiled=True)
    part, mixed = project(features, weight, causal)
    convolved = lax.psum_scatter(mixed, "tensor", scatter_dimension=0, tiled=True)
    return features, mixes, part, convolved


def backward_half(xin, cot, mixes, part, convolved, weight, ahead):
    grads, returned, taps = back(mixes, part, weight, ahead)
    returned = exchange(returned.reshape(-1, xin.shape[0], returned.shape[1]))
    return grads, taps, finish(xin, cot, convolved, returned)


def per_device(weights, filters, down_input, down_cot, up_input, up_cot):
    sections = lax.axis_size("section")
    mirror = [(s, sections - 1 - s) for s in range(sections)]
    down_pairs = [(s + 1, s) for s in range(sections - 1)]
    up_pairs = [(sections - s, s) for s in range(1, sections)]
    weight = weights[0]
    down = (down_input[0], down_cot[0])
    up = (lax.ppermute(up_input[0], "section", mirror), lax.ppermute(up_cot[0], "section", mirror))
    causal, ahead = toeplitz(filters[0])

    down_x, down_mixes, down_part, down_conv = forward_half(*down, weight, causal)
    up_x, up_mixes, up_part, up_conv = forward_half(*up, weight, causal)
    down_g, down_taps, down_grad = backward_half(
        *down, down_mixes, down_part, down_conv, weight, ahead
    )
    down_passed = lax.ppermute(down_grad, "section", down_pairs)
    up_g, up_taps, up_grad = backward_half(*up, up_mixes, up_part, up_conv, weight, ahead)
    up_passed = lax.ppermute(up_grad, "section", up_pairs)
    weight_grad = weight_gradient(down_x, up_x, down_g, up_g)
    taps = lax.psum((down_taps + up_taps).reshape(filters.shape[1:]), "tensor")
    return weight_grad[None], taps[None], down_passed[None], up_passed[None]


def solution(mesh):
    rows = P("section", "tensor", None)
    whole = P("section", None, None)
    return jax.shard_map(
        per_device,
        mesh=mesh,
        in_specs=(rows, whole, rows, rows, rows, rows),
        out_specs=(rows, whole, rows, rows),
        check_vma=False,
    )
```

time: 741 us -> 475 us (0.64); the launches traced: 726 us -> 470 us
  matrix products: 149 us -> 0 us
  local copies, waits for them, and re-layouts: 141 us -> 42 us
  other arithmetic: 86.3 us -> 0.01 us
  waiting for transfers between devices: 155 us -> 237 us
  Pallas kernels: 0 us -> 75.5 us
  blocking collectives: 130 us -> 74.1 us
  starting transfers between devices: 50.2 us -> 27.9 us
    dot_general x16 -> x0, matrix products: 149 us -> none  [the longest x2 27.8 us: banded(): jnp.einsum('tuk,gk->gtu', table, filter_taps, precision=lax.Precision.HIG...]
    reduce_scatter x2, waiting for transfers between devices: 0.01 us -> 121 us  [forward_half(): lax.psum_scatter(mixed, 'tensor', scatter_dimension=0, tiled=True)]
    pallas_call x0 -> x10, Pallas kernels: none -> 75.5 us  [the longest x2 29 us: back(): pl.pallas_call(back_kernel, grid=(groups // step,), in_specs=[spec, spec,...]
    ppermute x6 -> x4, waiting for transfers between devices: 110 us -> 46.4 us  [the longest x1 23.9 us: per_device(): lax.ppermute(up_input[0], 'section', mirror)]
    all_to_all x2 -> x1, blocking collectives: 115 us -> 58.8 us  [exchange(): return lax.all_to_all(x, 'tensor', split_axis=0, concat_axis=0, tiled=True)]
    unnamed x2 -> x0, other arithmetic: 48.9 us -> none
    all_to_all x6 -> x3, waiting for transfers between devices: 44.8 us -> 69.4 us  [exchange(): return lax.all_to_all(x, 'tensor', split_axis=0, concat_axis=0, tiled=True)]
    convert_element_type x5 -> x0, local copies, waits for them, and re-layouts: 22.3 us -> none  [the longest x2 12.2 us: layer_grads(): back_tokens = lax.all_to_all(returned_rows.astype(jnp.bfloat16), 'tensor'...]
  transfers between devices with their start and end apart: 16 -> 11, of which waited for: 5 -> 6; matrix products, arithmetic and copies ran while one was open for 48% -> 0% of each run, Pallas kernels for 0% -> 16%
where the time goes in v1:
time: 475 us; the launch traced here: 470 us
  waiting for transfers between devices  237 us (50%)
  Pallas kernels  75.5 us (16%)
  blocking collectives  74.1 us (16%)
  local copies, waits for them, and re-layouts  42 us (9%)
  starting transfers between devices  27.9 us (6%)
  between operations  13.9 us (3%)
    reduce_scatter x2, waiting for transfers between devices, forward_half(): lax.psum_scatter(mixed, 'tensor', scatter_dimension=0, tiled=True)  121 us
    all_to_all x3, waiting for transfers between devices, exchange(): return lax.all_to_all(x, 'tensor', split_axis=0, concat_axis=0, tiled=True)  69.4 us
    all_to_all x1, blocking collectives, exchange(): return lax.all_to_all(x, 'tensor', split_axis=0, concat_axis=0, tiled=True)  58.8 us
    unnamed x60, local copies, waits for them, and re-layouts  42 us
    pallas_call x2, Pallas kernels, back(): pl.pallas_call(back_kernel, grid=(groups // step,), in_specs=[spec, spec,...  29 us
    ppermute x1, waiting for transfers between devices, per_device(): lax.ppermute(up_input[0], 'section', mirror)  23.9 us
    ppermute x1, waiting for transfers between devices, per_device(): lax.ppermute(up_cot[0], 'section', mirror)  22.5 us
    pallas_call x2, Pallas kernels, project(): pl.pallas_call(project_kernel, grid=(groups // step,), in_specs=[pl.Block...  21 us
  transfers between devices with their start and end apart: 11, of which 6 were waited for; matrix products, arithmetic and copies ran while one was open for 0% of the time, Pallas kernels for 16%

profile of v1, /device:TPU:10, one launch (start us, length us, event | category | flops | bytes accessed | tf_op | source)
XLA Modules:
  0.0 470.4 jit_solution(13931955558372399623)
XLA Ops:
  9.7 2.2 prepare.2
  14.7 23.9 %collective-permute-done.xin_ref = bf16[128,4096]{1,0:T(8,128)(2,1)S(1)} collective-permute-done((bf16[128,4096]{1,0:T(8,128)(2,1)}, bf16[128,4096]{1,0:T(8,128)(2,1)S(1)}, u32[]{:S(2)}, u32[]{:S(2)}) %collective-permute-start) | collective-permute-done | bytes 1048608 | tf_op jit(solution)/shard_map/ppermute | solution.py:276
  38.6 22.5 %collective-permute-done.1.cot_ref = bf16[128,4096]{1,0:T(8,128)(2,1)S(1)} collective-permute-done((bf16[128,4096]{1,0:T(8,128)(2,1)}, bf16[128,4096]{1,0:T(8,128)(2,1)S(1)}, u32[]{:S(2)}, u32[]{:S(2)}) %collective-permute-start.1) | collective-permute-done | bytes 1048608 | tf_op jit(solution)/shard_map/ppermute | solution.py:276
  61.1 2.2 prepare.3
  65.3 5.3 %all-to-all-start = ((bf16[4,128,1024]{2,1,0:T(8,128)(2,1)}), bf16[4,128,1024]{2,1,0:T(8,128)(2,1)S(1)}, u32[]{:S(2)}, u32[]{:S(2)}) async-start(bf16[4,128,1024]{2,1,0:T(8,128)(2,1)} %get-tuple-element.20), calls=%async_computation | async-start | bytes 2097152 | tf_op jit(solution)/shard_map/all_to_all | solution.py:249
  73.4 39.1 %all-to-all-done = bf16[4,128,1024]{2,1,0:T(8,128)(2,1)S(1)} async-done(((bf16[4,128,1024]{2,1,0:T(8,128)(2,1)}), bf16[4,128,1024]{2,1,0:T(8,128)(2,1)S(1)}, u32[]{:S(2)}, u32[]{:S(2)}) %all-to-all-start) | async-done | bytes 1048608 | tf_op jit(solution)/shard_map/all_to_all | solution.py:249
  112.6 10.5 %project.2 = (bf16[512,4096]{1,0:T(8,128)(2,1)S(1)}, bf16[512,4096]{1,0:T(8,128)(2,1)S(1)}) custom-call(bf16[512,1024]{1,0:T(8,128)(2,1)S(1)} %bitcast.14, bf16[1024,4096]{1,0:T(8,128)(2,1)} %bitcast.24, bf16[32,128,256]{2,1,0:T(8,128)(2,1)S(1)} %get-tuple-element.23.causal_ref), custom_call_target="tpu_custom_call" | custom-call | tf_op jit(solution)/shard_map/project/pallas_call | solution.py:102
  123.1 2.0 copy-done.13
  125.1 2.0 copy-done.22
  128.3 58.8 %all_to_all.20 = bf16[4,128,1024]{2,1,0:T(8,128)(2,1)S(1)} all-to-all(bf16[4,128,1024]{2,1,0:T(8,128)(2,1)S(1)} %copy-done.26), channel_id=1, replica_groups=mesh['section'=8,'tensor'=4] {'tensor'}, dimensions={0} | all-to-all | bytes 2097152 | tf_op jit(solution)/shard_map/all_to_all | solution.py:249
  188.8 10.5 %project.3 = (bf16[512,4096]{1,0:T(8,128)(2,1)S(1)}, bf16[512,4096]{1,0:T(8,128)(2,1)S(1)}) custom-call(bf16[512,1024]{1,0:T(8,128)(2,1)S(1)} %bitcast.16, bf16[1024,4096]{1,0:T(8,128)(2,1)} %bitcast.25, bf16[32,128,256]{2,1,0:T(8,128)(2,1)S(1)} %copy-done.4), custom_call_target="tpu_custom_call" | custom-call | tf_op jit(solution)/shard_map/project/pallas_call | solution.py:102
  199.3 2.0 copy-done.14
  201.3 2.0 copy-done.21
  204.9 2.2 copy-done.15
  207.1 14.9 %back.2 = (bf16[512,4096]{1,0:T(8,128)(2,1)S(1)}, bf16[512,1024]{1,0:T(8,128)(2,1)}, f32[8,4,128]{2,1,0:T(4,128)S(1)}) custom-call(bf16[512,4096]{1,0:T(8,128)(2,1)S(1)} %copy-done.15, bf16[512,4096]{1,0:T(8,128)(2,1)} %copy-done.22, bf16[1024,4096]{1,0:T(8,128)(2,1)} %bitcast.26, bf16[32,128,256]{2,1,0:T(8,128)(2,1)S(1)} %copy-done.1), custom_call_target="tpu_custom_call" | custom-call | tf_op jit(solution)/shard_map/back/pallas_call | solution.py:169
  222.0 2.0 copy-done.17
  224.0 7.0 %all-to-all-start.2 = ((bf16[4,128,1024]{2,1,0:T(8,128)(2,1)}), bf16[4,128,1024]{2,1,0:T(8,128)(2,1)}, u32[]{:S(2)}, u32[]{:S(2)}) async-start(bf16[4,128,1024]{2,1,0:T(8,128)(2,1)} %bitcast.10), calls=%async_computation.3 | async-start | bytes 2097152 | tf_op jit(solution)/shard_map/all_to_all | solution.py:249
  232.6 2.2 copy-done.16
  234.8 14.1 %back.3 = (bf16[512,4096]{1,0:T(8,128)(2,1)S(1)}, bf16[512,1024]{1,0:T(8,128)(2,1)S(1)}, f32[8,4,128]{2,1,0:T(4,128)S(1)}) custom-call(bf16[512,4096]{1,0:T(8,128)(2,1)S(1)} %copy-done.16, bf16[512,4096]{1,0:T(8,128)(2,1)} %copy-done.21, bf16[1024,4096]{1,0:T(8,128)(2,1)} %bitcast.27, bf16[32,128,256]{2,1,0:T(8,128)(2,1)S(1)} %copy-done.2), custom_call_target="tpu_custom_call" | custom-call | tf_op jit(solution)/shard_map/back/pallas_call | solution.py:169
  251.9 30.3 %all-to-all-done.2.back_ref = bf16[4,128,1024]{2,1,0:T(8,128)(2,1)} async-done(((bf16[4,128,1024]{2,1,0:T(8,128)(2,1)}), bf16[4,128,1024]{2,1,0:T(8,128)(2,1)}, u32[]{:S(2)}, u32[]{:S(2)}) %all-to-all-start.2) | async-done | bytes 1048608 | tf_op jit(solution)/shard_map/all_to_all | solution.py:249
  282.2 7.4 %all-to-all-start.3 = ((bf16[4,128,1024]{2,1,0:T(8,128)(2,1)}), bf16[4,128,1024]{2,1,0:T(8,128)(2,1)}, u32[]{:S(2)}, u32[]{:S(2)}) async-start(bf16[4,128,1024]{2,1,0:T(8,128)(2,1)} %bitcast.22), calls=%async_computation.5 | async-start | bytes 2097152 | tf_op jit(solution)/shard_map/all_to_all | solution.py:249
  289.6 51.5 %reduce-scatter.3.cloned.1.call-done.mixed_ref = bf16[128,4096]{1,0:T(8,128)(2,1)} async-done(((bf16[512,4096]{1,0:T(8,128)(2,1)}), bf16[128,4096]{1,0:T(8,128)(2,1)}) %reduce-scatter.3.cloned.1.call-update) | async-done | bytes 1048592 | tf_op jit(solution)/shard_map/reduce_scatter | solution.py:259
  343.5 4.1 finish.2
  347.6 2.0 collective-permute-start.2
  349.6 69.6 %reduce-scatter.5.cloned.1.call-done.mixed_ref = bf16[128,4096]{1,0:T(8,128)(2,1)} async-done(((bf16[512,4096]{1,0:T(8,128)(2,1)}), bf16[128,4096]{1,0:T(8,128)(2,1)}) %reduce-scatter.5.cloned.1.call-update) | async-done | bytes 1048592 | tf_op jit(solution)/shard_map/reduce_scatter | solution.py:259
  422.9 3.2 finish.3
  426.1 3.4 collective-permute-start.3
  429.5 2.2 copy-done.20
  431.7 12.3 %weight_gradient.1 = bf16[1024,4096]{1,0:T(8,128)(2,1)} custom-call(bf16[512,1024]{1,0:T(8,128)(2,1)S(1)} %bitcast.15, bf16[512,1024]{1,0:T(8,128)(2,1)S(1)} %bitcast.17, bf16[512,4096]{1,0:T(8,128)(2,1)S(1)} %copy-done.18, bf16[512,4096]{1,0:T(8,128)(2,1)S(1)} %copy-done.20), custom_call_target="tpu_custom_call" | custom-call | tf_op jit(solution)/shard_map/weight_gradient/pallas_call | solution.py:209
  444.0 15.2 %psum.7 = f32[1,32,128]{2,1,0:T(8,128)} all-reduce(f32[1,32,128]{2,1,0:T(8,128)S(1)} %bitcast.29), channel_id=1, replica_groups=mesh['section'=8,'tensor'=4] {'tensor'}, use_global_device_ids=true, to_apply=%region_0.0 | all-reduce | flops 4096 | bytes 32768 | tf_op jit(solution)/shard_map/psum | solution.py:288
  459.3 2.3 copy.12
  461.5 2.3 copy.13
  (67 shorter events, 25.2 us)
Async XLA Ops:
  7.2 196.2 %all-gather.3.cloned.1.call-start = ((), (), s32[]{:S(2)}) async-start(), calls=%async_computation.6 | async-start | bytes 5242880 | tf_op jit(solution)/shard_map/all_gather | solution.py:257
  7.2 1.2 copy-start.5
  8.4 1.2 copy-start.7
  9.7 61.0 %copy-start.28 = (f32[1,32,128]{2,1,0:T(8,128)S(1)}, f32[1,32,128]{2,1,0:T(8,128)}, u32[]{:S(2)}) copy-start(f32[1,32,128]{2,1,0:T(8,128)} %param.7) | copy-start | bytes 49156
  11.9 219.1 %all-gather.5.cloned.1.call-start = ((), (), s32[]{:S(2)}) async-start(), calls=%async_computation.7 | async-start | bytes 5242880 | tf_op jit(solution)/shard_map/all_gather | solution.py:257
  12.0 26.6 %collective-permute-start = (bf16[128,4096]{1,0:T(8,128)(2,1)}, bf16[128,4096]{1,0:T(8,128)(2,1)S(1)}, u32[]{:S(2)}, u32[]{:S(2)}) collective-permute-start(bf16[128,4096]{1,0:T(8,128)(2,1)} %bitcast.30), channel_id=1, source_target_pairs={{0,28},{4,24},{8,20},{12,16},{16,12},{20,8},{24,4},{28,0},{1,29},{... | collective-permute-start | bytes 3145736 | tf_op jit(solution)/shard_map/ppermute | solution.py:276
  13.0 48.1 %collective-permute-start.1 = (bf16[128,4096]{1,0:T(8,128)(2,1)}, bf16[128,4096]{1,0:T(8,128)(2,1)S(1)}, u32[]{:S(2)}, u32[]{:S(2)}) collective-permute-start(bf16[128,4096]{1,0:T(8,128)(2,1)} %bitcast.31), channel_id=1, source_target_pairs={{0,28},{4,24},{8,20},{12,16},{16,12},{20,8},{24,4},{28,0},{1,29},{... | collective-permute-start | bytes 3145736 | tf_op jit(solution)/shard_map/ppermute | solution.py:276
  61.1 2.2 copy-start.11
  65.3 47.3 %all-to-all-start = ((bf16[4,128,1024]{2,1,0:T(8,128)(2,1)}), bf16[4,128,1024]{2,1,0:T(8,128)(2,1)S(1)}, u32[]{:S(2)}, u32[]{:S(2)}) async-start(bf16[4,128,1024]{2,1,0:T(8,128)(2,1)} %get-tuple-element.20), calls=%async_computation | async-start | bytes 2097152 | tf_op jit(solution)/shard_map/all_to_all | solution.py:249
  70.6 270.4 %reduce-scatter.3.cloned.1.call-start = ((), (), s32[]{:S(2)}) async-start(), calls=%async_computation.8 | async-start | bytes 5242880 | tf_op jit(solution)/shard_map/reduce_scatter | solution.py:259
  72.1 1.4 copy-start
  73.4 49.6 %copy-start.3 = (bf16[32,128,256]{2,1,0:T(8,128)(2,1)}, bf16[32,128,256]{2,1,0:T(8,128)(2,1)S(1)}, u32[]{:S(2)}) copy-start(bf16[32,128,256]{2,1,0:T(8,128)(2,1)S(1)} %get-tuple-element.23.causal_ref) | copy-start | bytes 6291460
  123.1 2.0 copy-start.13
  125.1 2.0 copy-start.22
  127.1 292.1 %reduce-scatter.5.cloned.1.call-start = ((), (), s32[]{:S(2)}) async-start(), calls=%async_computation.9 | async-start | bytes 5242880 | tf_op jit(solution)/shard_map/reduce_scatter | solution.py:259
  187.2 1.6 copy-start.4
  199.3 2.0 copy-start.14
  201.3 2.0 copy-start.21
  203.3 1.6 copy-start.1
  204.9 2.2 copy-start.15
  222.0 2.0 copy-start.17
  224.0 58.1 %all-to-all-start.2 = ((bf16[4,128,1024]{2,1,0:T(8,128)(2,1)}), bf16[4,128,1024]{2,1,0:T(8,128)(2,1)}, u32[]{:S(2)}, u32[]{:S(2)}) async-start(bf16[4,128,1024]{2,1,0:T(8,128)(2,1)} %bitcast.10), calls=%async_computation.3 | async-start | bytes 2097152 | tf_op jit(solution)/shard_map/all_to_all | solution.py:249
  231.0 1.6 copy-start.2
  232.6 2.2 copy-start.16
  234.8 106.3 %copy-start.6 = (bf16[1,128,4096]{2,1,0:T(8,128)(2,1)S(1)}, bf16[1,128,4096]{2,1,0:T(8,128)(2,1)}, u32[]{:S(2)}) copy-start(bf16[1,128,4096]{2,1,0:T(8,128)(2,1)} %param.8) | copy-start | bytes 3145732
  248.9 2.0 copy-start.19
  282.2 67.4 %all-to-all-start.3 = ((bf16[4,128,1024]{2,1,0:T(8,128)(2,1)}), bf16[4,128,1024]{2,1,0:T(8,128)(2,1)}, u32[]{:S(2)}, u32[]{:S(2)}) async-start(bf16[4,128,1024]{2,1,0:T(8,128)(2,1)} %bitcast.22), calls=%async_computation.5 | async-start | bytes 2097152 | tf_op jit(solution)/shard_map/all_to_all | solution.py:249
  341.1 1.2 copy-start.8
  347.6 111.6 %collective-permute-start.2 = (bf16[128,4096]{1,0:T(8,128)(2,1)}, bf16[128,4096]{1,0:T(8,128)(2,1)}, u32[]{:S(2)}, u32[]{:S(2)}) collective-permute-start(bf16[128,4096]{1,0:T(8,128)(2,1)} %finish.2), channel_id=1, source_target_pairs={{4,0},{8,4},{12,8},{16,12},{20,16},{24,20},{28,24},{5,1},{9,5},{13... | collective-permute-start | bytes 3145736 | tf_op jit(solution)/shard_map/ppermute | solution.py:284
  422.9 6.6 %copy-start.18 = (bf16[512,4096]{1,0:T(8,128)(2,1)S(1)}, bf16[512,4096]{1,0:T(8,128)(2,1)}, u32[]{:S(2)}) copy-start(bf16[512,4096]{1,0:T(8,128)(2,1)} %copy-done.17) | copy-start | bytes 12582916
  426.1 33.1 %collective-permute-start.3 = (bf16[128,4096]{1,0:T(8,128)(2,1)S(1)}, bf16[128,4096]{1,0:T(8,128)(2,1)}, u32[]{:S(2)}, u32[]{:S(2)}) collective-permute-start(bf16[128,4096]{1,0:T(8,128)(2,1)S(1)} %finish.3), channel_id=1, source_target_pairs={{28,4},{24,8},{20,12},{16,16},{12,20},{8,24},{4,28},{29,5},{25,9},... | collective-permute-start | bytes 3145736 | tf_op jit(solution)/shard_map/ppermute | solution.py:286
  429.5 2.2 copy-start.20
  (8 other events, 9.1 us)
Sparse Core Ops, SparseCore 0:
  12.0 99.6 all-gather.2
  113.3 101.6 all-gather.4
  217.2 123.8 reduce-scatter.2
  343.3 75.8 reduce-scatter.4
